TPU v7x, 32 devices: a whole 2x2x4 slice. The times are simulated.
32 devices in a mesh: ctx: 8 (over y, x, core), exp: 4 (over z).
Axes of the slice: x: 2, y: 2, z: 4, core: 2. Of those that a mesh axis runs over, the one named last changes fastest.
Arguments:
- mixer_x: bfloat16 [1024, 4096], P('ctx', 'exp')
- mixer_z: bfloat16 [1024, 4096], P('ctx', 'exp'), may hold values from -6 to 6
- step_raw: float32 [1024, 4096], P('ctx', 'exp')
- input_b: float32 [16, 1024], P(None, 'ctx'), may hold values from -6 to 6
- output_c: float32 [16, 1024], P(None, 'ctx'), may hold values from -4 to 4
- decay_log: float32 [16, 4096], P(None, 'exp')
- skip_gain: float32 [4096], P('exp'), may hold values from 0.5 to 1.5
- out_proj: bfloat16 [4096, 2048], P('exp'), may hold values from -0.09375 to 0.09375
- residual: bfloat16 [1024, 2048], P(('ctx', 'exp')), may hold values from -6 to 6
- norm_gain: float32 [2048], replicated, may hold values from 0.1 to 1.9
- gate_proj: bfloat16 [4, 2048, 8192], P('exp', None, 'ctx'), may hold values from -0.125 to 0.125
- up_proj: bfloat16 [4, 2048, 8192], P('exp', None, 'ctx'), may hold values from -0.125 to 0.125
- down_proj: bfloat16 [4, 8192, 2048], P('exp', 'ctx'), may hold values from -0.0625 to 0.0625
- expert_ids: int32 [1024, 2], P(('ctx', 'exp')), may hold values from 0 to 3, as said below
- slot_ids: int32 [1024, 2], P(('ctx', 'exp')), may hold values from -1 to 15, as said below
- route_weight: float32 [1024, 2], P(('ctx', 'exp')), may hold values from 0.2 to 1
Outputs:
- layer_out: bfloat16 [1024, 2048], P(('ctx', 'exp'))
Inputs may be any that keep to these rules, and one draw needn't show every extreme that they name: `expert_ids`: A token's two ids differ. In every draw one expert is named by at least 16 tokens of every device's 32 tokens. `slot_ids`: A copy's slot is its rank among the copies of the same device's tokens to the same expert, taken in order of token and then of choice, or -1 where that rank is 16 or more.
All inputs are finite; a program needn't handle non-finite values.
Results may differ from a plain program's by a relative error of at most 0.017.
Values may be sent and summed in bfloat16 or wider, within the bound.
A program may use at most 64 MiB of HBM per device.

v0:
```python
import jax
import jax.numpy as jnp
from jax import lax
from jax.sharding import PartitionSpec as P

EPSILON = 1e-05


def prefix(array, axis, combine, identity):
    count, here = (lax.axis_size(axis), lax.axis_index(axis))
    everything = jax.tree.map(
        lambda part, kind: lax.all_gather(part.astype(kind), axis),
        array,
        (jnp.bfloat16, jnp.bfloat16),
    )
    start = jax.tree.map(
        lambda part, zero: jnp.broadcast_to(jnp.asarray(zero, part.dtype), part.shape),
        array,
        identity,
    )

    def lap(k, before):
        reached = k < here
        new = combine(
            before, jax.tree.map(lambda part, own: part[k].astype(own.dtype), everything, array)
        )
        return jax.tree.map(lambda a, b: jnp.where(reached, a, b), new, before)

    return lax.fori_loop(0, count, lap, start)


def link_states(earlier, later):
    return (earlier[0] * later[0], later[0] * earlier[1] + later[1])


def local_recurrence(step_size, x_float, input_b, output_c, decay_rate):
    tokens = step_size.shape[0]
    width = step_size.shape[1]
    states = decay_rate.shape[0]
    sub_len = tokens // 16
    step_blocks = step_size.reshape(16, sub_len, width)
    x_blocks = x_float.reshape(16, sub_len, width)
    b_blocks = input_b.T.reshape(16, sub_len, states)
    c_blocks = output_c.T.reshape(16, sub_len, states)

    def advance(carry, blocks):
        state, run_step = carry
        step_blk, x_blk, b_blk, c_blk = blocks
        outputs = []
        totals = []
        for inner_pos in range(sub_len):
            step_now = step_blk[inner_pos]
            state = (
                jnp.exp(step_now[None, :] * decay_rate) * state
                + (step_now * x_blk[inner_pos])[None, :] * b_blk[inner_pos][:, None]
            )
            run_step = run_step + step_now
            outputs.append(jnp.sum(c_blk[inner_pos][:, None] * state, axis=0))
            totals.append(run_step)
        return ((state, run_step), (jnp.stack(outputs), jnp.stack(totals)))

    start = (jnp.zeros((states, width), jnp.float32), jnp.zeros((width,), jnp.float32))
    finals, outs = lax.scan(advance, start, (step_blocks, x_blocks, b_blocks, c_blocks))
    local_y = outs[0].reshape(tokens, width)
    cumulative = outs[1].reshape(tokens, width)
    return (finals[0], finals[1], local_y, cumulative)


def on_device(
    mixer_x,
    mixer_z,
    step_raw,
    input_b,
    output_c,
    decay_log,
    skip_gain,
    out_proj,
    residual,
    norm_gain,
    gate_proj,
    up_proj,
    down_proj,
    expert_ids,
    slot_ids,
    route_weight,
):
    n_exp = lax.axis_size("exp")
    step_size = jax.nn.softplus(step_raw)
    decay_rate = -jnp.exp(decay_log)
    x_float = mixer_x.astype(jnp.float32)
    final_state, total_step, local_y, cumulative = local_recurrence(
        step_size, x_float, input_b, output_c, decay_rate
    )
    through_final = jnp.exp(total_step[None, :] * decay_rate)
    identity = (jnp.ones_like(through_final), jnp.zeros_like(final_state))
    carried = prefix((through_final, final_state), "ctx", link_states, identity)
    carried_state = carried[1]
    correction = jnp.zeros_like(local_y)
    for state_index in range(decay_rate.shape[0]):
        weight_row = (
            jnp.exp(cumulative * decay_rate[state_index][None, :])
            * carried_state[state_index][None, :]
        )
        correction = correction + output_c[state_index][:, None] * weight_row
    mixer_y = local_y + correction + skip_gain * x_float
    gated = (mixer_y * jax.nn.silu(mixer_z.astype(jnp.float32))).astype(jnp.bfloat16)
    partial_out = jnp.dot(gated, out_proj, preferred_element_type=jnp.float32)
    tok_dev = residual.shape[0]
    model_width = residual.shape[1]
    summed = lax.psum(partial_out.astype(jnp.bfloat16), "exp").astype(jnp.float32)
    mixer_out = lax.dynamic_slice_in_dim(summed, lax.axis_index("exp") * tok_dev, tok_dev, 0)
    hidden_one = (residual.astype(jnp.float32) + mixer_out).astype(jnp.bfloat16)
    hidden_one = lax.optimization_barrier(hidden_one)
    hidden_float = hidden_one.astype(jnp.float32)
    inv_rms = lax.rsqrt(jnp.mean(hidden_float * hidden_float, axis=-1, keepdims=True) + EPSILON)
    normed = (hidden_float * inv_rms * norm_gain).astype(jnp.bfloat16)
    experts_local = gate_proj.shape[0]
    experts_all = experts_local * n_exp
    capacity = max(2, expert_ids.shape[1] * tok_dev // experts_all)
    slot_count = experts_all * capacity
    per_device = experts_local * capacity
    target_index = jnp.where(slot_ids >= 0, expert_ids * capacity + slot_ids, -1)
    slot_iota = jnp.arange(slot_count, dtype=jnp.int32)
    select = jnp.any(target_index[None, :, :] == slot_iota[:, None, None], axis=-1).astype(
        jnp.bfloat16
    )
    dispatch = jnp.dot(select, normed, preferred_element_type=jnp.float32).astype(jnp.bfloat16)
    arrived = lax.all_to_all(
        dispatch.reshape(n_exp, per_device, model_width),
        "exp",
        split_axis=0,
        concat_axis=0,
        tiled=True,
    )
    piece = lax.all_gather(arrived, "ctx", axis=0, tiled=True)
    outputs = []
    local_index = 0
    rows_here = piece.reshape(-1, piece.shape[2])
    gate_value = jnp.dot(rows_here, gate_proj[local_index], preferred_element_type=jnp.float32)
    up_value = jnp.dot(rows_here, up_proj[local_index], preferred_element_type=jnp.float32)
    hidden = (jax.nn.silu(gate_value) * up_value).astype(jnp.bfloat16)
    outputs.append(hidden.reshape(piece.shape[0], capacity, hidden.shape[1]))
    hidden_rows = outputs[0]
    outputs = []
    local_index = 0
    rows_here = hidden_rows.reshape(-1, hidden_rows.shape[2])
    product = jnp.dot(rows_here, down_proj[local_index], preferred_element_type=jnp.float32)
    outputs.append(product.reshape(n_exp * lax.axis_size("ctx"), capacity, model_width))
    expert_out = lax.psum_scatter(
        outputs[0].astype(jnp.bfloat16), "ctx", scatter_dimension=0, tiled=True
    )
    returned = lax.all_to_all(expert_out, "exp", split_axis=0, concat_axis=0, tiled=True).reshape(
        slot_count, model_width
    )
    matches = target_index[:, :, None] == slot_iota[None, None, :]
    combine = jnp.sum(
        jnp.where(matches, route_weight[:, :, None], jnp.zeros_like(route_weight)[:, :, None]),
        axis=1,
    )
    moe_out = jnp.dot(combine, returned.astype(jnp.float32), precision=lax.Precision.HIGHEST)
    return (hidden_float + moe_out).astype(jnp.bfloat16)


def solution(mesh):
    placed = (
        P("ctx", "exp"),
        P("ctx", "exp"),
        P("ctx", "exp"),
        P(None, "ctx"),
        P(None, "ctx"),
        P(None, "exp"),
        P("exp"),
        P("exp", None),
        P(("ctx", "exp"), None),
        P(),
        P("exp", None, "ctx"),
        P("exp", None, "ctx"),
        P("exp", "ctx", None),
        P(("ctx", "exp"), None),
        P(("ctx", "exp"), None),
        P(("ctx", "exp"), None),
    )
    return jax.shard_map(
        on_device, mesh=mesh, in_specs=placed, out_specs=P(("ctx", "exp"), None), check_vma=False
    )
```

profile of v0, /device:TPU:0, one launch (start us, length us, event | category | flops | bytes accessed | tf_op | source)
XLA Modules:
  0.0 205.2 jit_solution(5551518412730478599)
XLA Ops:
  6.5 0.9 exponential_negate_fusion
  7.4 1.0 convert_bitcast_fusion
  8.4 1.3 fusion.20
  9.7 0.8 copy.27
  10.5 1.0 slice_bitcast_fusion.31
  11.6 0.8 copy.28
  12.4 13.4 %while.31 = (s32[]{:T(128)}, f32[16,1024]{1,0:T(8,128)S(1)}, f32[1024]{0:T(1024)S(1)}, f32[16,8,1024]{2,1,0:T(8,128)S(1)}, f32[16,8,1024]{2,1,0:T(8,128)S(1)}, /...) while((s32[]{:T(128)}, f32[16,1024]{1,0:T(8,128)S(1)}, ...), condition=%wide.region_9.10_spmd.clone, body=%wide.region_0.9_spmd.clone.sunk | while | flops 1156106 | bytes 1459865 | solution.py:63
  12.7 0.2 multiply_reduce_fusion.11
  12.8 0.1 multiply_reduce_fusion.13
  13.5 0.2 multiply_reduce_fusion.11
  13.7 0.1 multiply_reduce_fusion.13
  14.3 0.2 multiply_reduce_fusion.11
  15.2 0.2 multiply_reduce_fusion.11
  15.3 0.1 multiply_reduce_fusion.13
  16.0 0.2 multiply_reduce_fusion.11
  16.2 0.1 multiply_reduce_fusion.13
  16.9 0.2 multiply_reduce_fusion.11
  17.7 0.2 multiply_reduce_fusion.11
  17.9 0.1 multiply_reduce_fusion.13
  18.5 0.2 multiply_reduce_fusion.11
  18.7 0.1 multiply_reduce_fusion.13
  19.4 0.2 multiply_reduce_fusion.11
  20.2 0.2 multiply_reduce_fusion.11
  20.4 0.1 multiply_reduce_fusion.13
  21.0 0.2 multiply_reduce_fusion.11
  21.9 0.2 multiply_reduce_fusion.11
  22.1 0.1 multiply_reduce_fusion.13
  22.7 0.2 multiply_reduce_fusion.11
  22.9 0.1 multiply_reduce_fusion.13
  23.6 0.2 multiply_reduce_fusion.11
  24.4 0.2 multiply_reduce_fusion.11
  25.2 0.2 multiply_reduce_fusion.11
  25.9 10.9 %all-gather = bf16[128,1024]{1,0:T(8,128)(2,1)S(1)} all-gather(bf16[16,1024]{1,0:T(8,128)(2,1)S(1)} %exponential_convert_fusion), channel_id=2, replica_groups=mesh['ctx'=8,'exp'=4] {'ctx'}, dimensions={0}, use_global_device_ids=true | all-gather | bytes 294912 | tf_op jit(solution)/shard_map/all_gather | solution.py:12
  36.8 9.3 %all-gather.1 = bf16[128,1024]{1,0:T(8,128)(2,1)S(1)} all-gather(bf16[16,1024]{1,0:T(8,128)(2,1)S(1)} %convert_element_type.70), channel_id=3, replica_groups=mesh['ctx'=8,'exp'=4] {'ctx'}, dimensions={0}, use_global_device_ids=true | all-gather | bytes 294912 | tf_op jit(solution)/shard_map/all_gather | solution.py:12
  46.1 0.4 while.32
  46.6 5.8 %convolution_convert_fusion = bf16[128,2048]{1,0:T(8,128)(2,1)} fusion(bf16[1024,2048]{1,0:T(8,128)(2,1)} %param.27, bf16[128,1024]{1,0:T(8,128)(2,1)S(1)} %copy-done, bf16[128,1024]{1,0:T(8,128)(2,1)S(1)} %copy-done.10, f32[16,8,1024]{2,1,0:T(8,128)S(1)} %get-tuple-element.155, f32[16,8,1024]{2,1,0:T(8,128)S(1)} %get-tuple-element.154, ...), kind=kOutput, calls=%fused_computation.64 | convolution fusion | flops 546832384 | bytes 6434816 | tf_op jit(solution)/shard_map/dot_general | solution.py:107
  52.6 38.6 %all-reduce.2.cloned.1.call-done = bf16[128,2048]{1,0:T(8,128)(2,1)} async-done(((bf16[128,2048]{1,0:T(8,128)(2,1)}), bf16[128,2048]{1,0:T(8,128)(2,1)}) %all-reduce.2.cloned.1.call-update) | async-done | bytes 524304 | tf_op jit(solution)/shard_map/psum | solution.py:110
  91.2 0.9 add_convert_fusion
  92.3 0.3 convolution_convert_fusion.1
  92.6 11.4 %all_to_all.10 = bf16[4,16,2048]{2,1,0:T(8,128)(2,1)} all-to-all(bf16[4,16,2048]{2,1,0:T(8,128)(2,1)S(1)} %bitcast.443), channel_id=1, replica_groups=mesh['ctx'=8,'exp'=4] {'exp'}, dimensions={0} | all-to-all | bytes 524288 | tf_op jit(solution)/shard_map/all_to_all | solution.py:128
  104.0 27.2 %all-gather.4.cloned.1.call-done = bf16[32,16,2048]{2,1,0:T(8,128)(2,1)} async-done(((bf16[4,16,2048]{2,1,0:T(8,128)(2,1)}), bf16[32,16,2048]{2,1,0:T(8,128)(2,1)}) %all-gather.4.cloned.1.call-update) | async-done | bytes 2097168 | tf_op jit(solution)/shard_map/all_gather | solution.py:135
  131.2 5.3 %fusion.6 = f32[512,1024]{1,0:T(8,128)S(1)} fusion(bf16[512,2048]{1,0:T(8,128)(2,1)} %bitcast.513, bf16[1,2048,1024]{2,1,0:T(8,128)(2,1)} %param.30), kind=kOutput, calls=%fused_computation.61 | convolution fusion | flops 2147483648 | bytes 8388608 | tf_op jit(solution)/shard_map/dot_general | solution.py:139
  136.6 2.5 %multiply_convert_fusion = bf16[512,1024]{1,0:T(8,128)(2,1)S(1)} fusion(f32[512,1024]{1,0:T(8,128)S(1)} %fusion.6, bf16[512,2048]{1,0:T(8,128)(2,1)S(1)} %bitcast.514, bf16[1,2048,1024]{2,1,0:T(8,128)(2,1)S(1)} %copy-done.7), kind=kOutput, calls=%fused_computation.68 | convolution fusion | flops 2150629376 | bytes 9437184 | tf_op jit(solution)/shard_map/dot_general | solution.py:140
  139.1 3.7 %fusion.8 = bf16[32,16,2048]{2,1,0:T(8,128)(2,1)} fusion(bf16[32,16,1024]{2,1,0:T(8,128)(2,1)S(1)} %bitcast.515, bf16[1,1024,2048]{2,1,0:T(8,128)(2,1)S(1)} %copy-done.8), kind=kOutput, calls=%fused_computation.63 | convolution fusion | flops 2148532224 | bytes 7340032 | tf_op jit(solution)/shard_map/dot_general | solution.py:147
  142.8 41.4 %reduce-scatter.2.cloned.1.call-done = bf16[4,16,2048]{2,1,0:T(8,128)(2,1)} async-done(((bf16[32,16,2048]{2,1,0:T(8,128)(2,1)}), bf16[4,16,2048]{2,1,0:T(8,128)(2,1)}) %reduce-scatter.2.cloned.1.call-update) | async-done | bytes 262160 | tf_op jit(solution)/shard_map/reduce_scatter | solution.py:149
  184.2 4.6 %all-to-all-start.1 = ((bf16[4,16,2048]{2,1,0:T(8,128)(2,1)}), bf16[4,16,2048]{2,1,0:T(8,128)(2,1)S(1)}, u32[]{:S(2)}, u32[]{:S(2)}) async-start(bf16[4,16,2048]{2,1,0:T(8,128)(2,1)} %reduce-scatter.2.cloned.1.call-done), calls=%async_computation.2 | async-start | bytes 524288 | tf_op jit(solution)/shard_map/all_to_all | solution.py:152
  188.9 8.8 %all-to-all-done.1 = bf16[4,16,2048]{2,1,0:T(8,128)(2,1)S(1)} async-done(((bf16[4,16,2048]{2,1,0:T(8,128)(2,1)}), bf16[4,16,2048]{2,1,0:T(8,128)(2,1)S(1)}, u32[]{:S(2)}, u32[]{:S(2)}) %all-to-all-start.1) | async-done | bytes 262176 | tf_op jit(solution)/shard_map/all_to_all | solution.py:152
  197.7 0.9 fusion.11
  (251 shorter events, 8.6 us)
Async XLA Ops:
  6.5 84.7 %all-reduce.2.cloned.1.call-start = ((), (), s32[]{:S(2)}) async-start(), calls=%async_computation.3 | async-start | bytes 1048576 | tf_op jit(solution)/shard_map/psum | solution.py:110
  12.4 13.5 %copy-start.1 = (f32[16,1024]{1,0:T(8,128)S(1)}, f32[16,1024]{1,0:T(8,128)}, u32[]{:S(2)}) copy-start(f32[16,1024]{1,0:T(8,128)} %param.25) | copy-start | bytes 196612
  25.9 20.7 %copy-start = (bf16[128,1024]{1,0:T(8,128)(2,1)S(1)}, bf16[128,1024]{1,0:T(8,128)(2,1)}, u32[]{:S(2)}) copy-start(bf16[128,1024]{1,0:T(8,128)(2,1)} %param.20) | copy-start | bytes 786436
  25.9 20.7 %copy-start.10 = (bf16[128,1024]{1,0:T(8,128)(2,1)S(1)}, bf16[128,1024]{1,0:T(8,128)(2,1)}, u32[]{:S(2)}) copy-start(bf16[128,1024]{1,0:T(8,128)(2,1)} %param.21) | copy-start | bytes 786436
  25.9 20.7 %copy-start.11 = (f32[1024]{0:T(1024)S(1)}, f32[1024]{0:T(1024)}, u32[]{:S(2)}) copy-start(f32[1024]{0:T(1024)} %param.26) | copy-start | bytes 12292
  46.6 5.9 %copy-start.4 = (s32[32,2]{0,1:T(2,128)S(1)}, s32[32,2]{0,1:T(2,128)}, u32[]{:S(2)}) copy-start(s32[32,2]{0,1:T(2,128)} %param.34) | copy-start | bytes 772
  46.6 5.9 %copy-start.5 = (s32[32,2]{0,1:T(2,128)S(1)}, s32[32,2]{0,1:T(2,128)}, u32[]{:S(2)}) copy-start(s32[32,2]{0,1:T(2,128)} %param.33) | copy-start | bytes 772
  46.6 44.6 %copy-start.2 = (bf16[32,2048]{1,0:T(8,128)(2,1)S(1)}, bf16[32,2048]{1,0:T(8,128)(2,1)}, u32[]{:S(2)}) copy-start(bf16[32,2048]{1,0:T(8,128)(2,1)} %param.28) | copy-start | bytes 393220
  46.6 45.7 %copy-start.3 = (f32[2048]{0:T(1024)S(1)}, f32[2048]{0:T(1024)}, u32[]{:S(2)}) copy-start(f32[2048]{0:T(1024)} %param.29) | copy-start | bytes 24580
  52.5 78.8 %all-gather.4.cloned.1.call-start = ((), (), s32[]{:S(2)}) async-start(), calls=%async_computation.4 | async-start | bytes 2359296 | tf_op jit(solution)/shard_map/all_gather | solution.py:135
  104.0 80.2 %reduce-scatter.2.cloned.1.call-start = ((), (), s32[]{:S(2)}) async-start(), calls=%async_computation.5 | async-start | bytes 2359296 | tf_op jit(solution)/shard_map/reduce_scatter | solution.py:149
  131.2 5.3 %copy-start.7 = (bf16[1,2048,1024]{2,1,0:T(8,128)(2,1)S(1)}, bf16[1,2048,1024]{2,1,0:T(8,128)(2,1)}, u32[]{:S(2)}) copy-start(bf16[1,2048,1024]{2,1,0:T(8,128)(2,1)} %param.31) | copy-start | bytes 12582916
  131.2 5.3 %copy-start.9 = (bf16[32,16,2048]{2,1,0:T(8,128)(2,1)S(1)}, bf16[32,16,2048]{2,1,0:T(8,128)(2,1)}, u32[]{:S(2)}) copy-start(bf16[32,16,2048]{2,1,0:T(8,128)(2,1)} %all-gather.4.cloned.1.call-done) | copy-start | bytes 6291460
  136.6 2.5 %copy-start.8 = (bf16[1,1024,2048]{2,1,0:T(8,128)(2,1)S(1)}, bf16[1,1024,2048]{2,1,0:T(8,128)(2,1)}, u32[]{:S(2)}) copy-start(bf16[1,1024,2048]{2,1,0:T(8,128)(2,1)} %param.32) | copy-start | bytes 12582916
  142.8 46.0 %copy-start.6 = (f32[32,2]{0,1:T(2,128)S(1)}, f32[32,2]{0,1:T(2,128)}, u32[]{:S(2)}) copy-start(f32[32,2]{0,1:T(2,128)} %param.35) | copy-start | bytes 772
  184.2 13.5 %all-to-all-start.1 = ((bf16[4,16,2048]{2,1,0:T(8,128)(2,1)}), bf16[4,16,2048]{2,1,0:T(8,128)(2,1)S(1)}, u32[]{:S(2)}, u32[]{:S(2)}) async-start(bf16[4,16,2048]{2,1,0:T(8,128)(2,1)} %reduce-scatter.2.cloned.1.call-done), calls=%async_computation.2 | async-start | bytes 524288 | tf_op jit(solution)/shard_map/all_to_all | solution.py:152
Sparse Core Ops, SparseCore 0:
  52.6 38.5 all-reduce.1
  104.1 27.0 all-gather.3
  143.0 41.1 reduce-scatter.1
where the time goes:
time: 206 us; the launch traced here: 205 us
  waiting for transfers between devices  116 us (56%)
  blocking collectives  31.6 us (15%)
  matrix products  18.6 us (9%)
  between operations  13.4 us (7%)
  other arithmetic  12.1 us (6%)
  local copies, waits for them, and re-layouts  7.03 us (3%)
  starting transfers between devices  4.69 us (2%)
    reduce_scatter x1, waiting for transfers between devices, on_device(): lax.psum_scatter(outputs[0].astype(jnp.bfloat16), 'ctx', scatter_dimensio...  41.4 us
    psum x1, waiting for transfers between devices, on_device(): lax.psum(partial_out.astype(jnp.bfloat16), 'exp').astype(jnp.float32)  38.6 us
    all_gather x1, waiting for transfers between devices, on_device(): piece = lax.all_gather(arrived, 'ctx', axis=0, tiled=True)  27.2 us
    all_gather x2, blocking collectives, prefix(): lax.all_gather(part.astype(kind), axis)  20.2 us
    all_to_all x1, blocking collectives, on_device(): lax.all_to_all(dispatch.reshape(n_exp, per_device, model_width), 'exp', s...  11.4 us
    all_to_all x1, waiting for transfers between devices, on_device(): lax.all_to_all(expert_out, 'exp', split_axis=0, concat_axis=0, tiled=True)  8.81 us
    reduce_sum x48, other arithmetic, advance(): outputs.append(jnp.sum(c_blk[inner_pos][:, None] * state, axis=0))  6.82 us
    dot_general x1, matrix products, on_device(): partial_out = jnp.dot(gated, out_proj, preferred_element_type=jnp.float32)  5.81 us
  transfers between devices with their start and end apart: 4, of which 4 were waited for; matrix products, arithmetic and copies ran while one was open for 0% of the time, Pallas kernels for 0%

commit v1 on v0

--- a/solution.py
+++ b/solution.py
@@ -132,7 +132,12 @@
         concat_axis=0,
         tiled=True,
     )
-    piece = lax.all_gather(arrived, "ctx", axis=0, tiled=True)
+    ring = [arrived]
+    for hop in range(7):
+        ring.append(lax.ppermute(ring[-1], "ctx", [(dev, (dev + 1) % 8) for dev in range(8)]))
+    piece = jnp.roll(
+        jnp.concatenate(ring[::-1], axis=0), (lax.axis_index("ctx") + 1) * ring[0].shape[0], axis=0
+    )
     outputs = []
     local_index = 0
     rows_here = piece.reshape(-1, piece.shape[2])

time: 206 us -> 223 us (1.083)
  waiting for transfers between devices: 116 us -> 134 us
  matrix products: 18.6 us -> 15.6 us
  local copies, waits for them, and re-layouts: 7.03 us -> 9.3 us
    ppermute x0 -> x7, waiting for transfers between devices: none -> 46.9 us  [on_device(): lax.ppermute(ring[-1], 'ctx', [(dev, (dev + 1) % 8) for dev in range(8)])]
    all_gather x1 -> x0, waiting for transfers between devices: 27.2 us -> none  [on_device(): piece = lax.all_gather(arrived, 'ctx', axis=0, tiled=True)]
    dot_general x1, matrix products: 5.29 us -> 2.35 us  [on_device(): jnp.dot(rows_here, gate_proj[local_index], preferred_element_type=jnp.flo...]
  transfers between devices with their start and end apart: 4 -> 10, of which waited for: 4 -> 10; matrix products, arithmetic and copies ran while one was open for 0% -> 0% of each run, Pallas kernels for 0% -> 0%
where the time goes in v1:
time: 223 us; the launch traced here: 222 us
  waiting for transfers between devices  134 us (60%)
  blocking collectives  30.8 us (14%)
  matrix products  15.6 us (7%)
  between operations  13.8 us (6%)
  other arithmetic  12.1 us (5%)
  local copies, waits for them, and re-layouts  9.3 us (4%)
  starting transfers between devices  4.66 us (2%)
    ppermute x7, waiting for transfers between devices, on_device(): lax.ppermute(ring[-1], 'ctx', [(dev, (dev + 1) % 8) for dev in range(8)])  46.9 us
    reduce_scatter x1, waiting for transfers between devices, on_device(): lax.psum_scatter(outputs[0].astype(jnp.bfloat16), 'ctx', scatter_dimensio...  39.8 us
    psum x1, waiting for transfers between devices, on_device(): lax.psum(partial_out.astype(jnp.bfloat16), 'exp').astype(jnp.float32)  38.6 us
    all_gather x2, blocking collectives, prefix(): lax.all_gather(part.astype(kind), axis)  20.1 us
    all_to_all x1, blocking collectives, on_device(): lax.all_to_all(dispatch.reshape(n_exp, per_device, model_width), 'exp', s...  10.7 us
    all_to_all x1, waiting for transfers between devices, on_device(): lax.all_to_all(expert_out, 'exp', split_axis=0, concat_axis=0, tiled=True)  8.85 us
    reduce_sum x48, other arithmetic, advance(): outputs.append(jnp.sum(c_blk[inner_pos][:, None] * state, axis=0))  6.82 us
    dot_general x1, matrix products, on_device(): partial_out = jnp.dot(gated, out_proj, preferred_element_type=jnp.float32)  5.79 us
  transfers between devices with their start and end apart: 10, of which 10 were waited for; matrix products, arithmetic and copies ran while one was open for 0% of the time, Pallas kernels for 0%

profile of v1, /device:TPU:0, one launch (start us, length us, event | category | flops | bytes accessed | tf_op | source)
XLA Modules:
  0.0 222.2 jit_solution(9386014605429007552)
XLA Ops:
  6.5 0.9 exponential_negate_fusion
  7.4 1.0 convert_bitcast_fusion
  8.4 1.3 fusion.20
  9.7 0.8 copy.22
  10.5 1.0 slice_bitcast_fusion.31
  11.6 0.8 copy.23
  12.5 13.4 %while.31 = (s32[]{:T(128)}, f32[16,1024]{1,0:T(8,128)S(1)}, f32[1024]{0:T(1024)S(1)}, f32[16,8,1024]{2,1,0:T(8,128)S(1)}, f32[16,8,1024]{2,1,0:T(8,128)S(1)}, /...) while((s32[]{:T(128)}, f32[16,1024]{1,0:T(8,128)S(1)}, ...), condition=%wide.region_9.10_spmd.clone, body=%wide.region_0.9_spmd.clone.sunk | while | flops 1156106 | bytes 1459865 | solution.py:63
  12.7 0.2 multiply_reduce_fusion.11
  12.9 0.1 multiply_reduce_fusion.13
  13.5 0.2 multiply_reduce_fusion.11
  14.4 0.2 multiply_reduce_fusion.11
  15.2 0.2 multiply_reduce_fusion.11
  16.1 0.2 multiply_reduce_fusion.11
  16.9 0.2 multiply_reduce_fusion.11
  17.7 0.2 multiply_reduce_fusion.11
  18.6 0.2 multiply_reduce_fusion.11
  19.4 0.2 multiply_reduce_fusion.11
  20.2 0.2 multiply_reduce_fusion.11
  21.1 0.2 multiply_reduce_fusion.11
  21.9 0.2 multiply_reduce_fusion.11
  22.8 0.2 multiply_reduce_fusion.11
  23.6 0.2 multiply_reduce_fusion.11
  24.4 0.2 multiply_reduce_fusion.11
  25.3 0.2 multiply_reduce_fusion.11
  25.9 10.8 %all-gather = bf16[128,1024]{1,0:T(8,128)(2,1)S(1)} all-gather(bf16[16,1024]{1,0:T(8,128)(2,1)S(1)} %exponential_convert_fusion), channel_id=2, replica_groups=mesh['ctx'=8,'exp'=4] {'ctx'}, dimensions={0}, use_global_device_ids=true | all-gather | bytes 294912 | tf_op jit(solution)/shard_map/all_gather | solution.py:12
  36.7 9.3 %all-gather.1 = bf16[128,1024]{1,0:T(8,128)(2,1)S(1)} all-gather(bf16[16,1024]{1,0:T(8,128)(2,1)S(1)} %convert_element_type.70), channel_id=3, replica_groups=mesh['ctx'=8,'exp'=4] {'ctx'}, dimensions={0}, use_global_device_ids=true | all-gather | bytes 294912 | tf_op jit(solution)/shard_map/all_gather | solution.py:12
  46.0 0.4 while.32
  46.5 5.8 %convolution_convert_fusion = bf16[128,2048]{1,0:T(8,128)(2,1)} fusion(bf16[1024,2048]{1,0:T(8,128)(2,1)} %param.27, bf16[128,1024]{1,0:T(8,128)(2,1)S(1)} %copy-done, bf16[128,1024]{1,0:T(8,128)(2,1)S(1)} %copy-done.10, f32[16,8,1024]{2,1,0:T(8,128)S(1)} %get-tuple-element.155, f32[16,8,1024]{2,1,0:T(8,128)S(1)} %get-tuple-element.154, ...), kind=kOutput, calls=%fused_computation.64 | convolution fusion | flops 546832384 | bytes 6434816 | tf_op jit(solution)/shard_map/dot_general | solution.py:107
  52.5 38.6 %all-reduce.2.cloned.1.call-done = bf16[128,2048]{1,0:T(8,128)(2,1)} async-done(((bf16[128,2048]{1,0:T(8,128)(2,1)}), bf16[128,2048]{1,0:T(8,128)(2,1)}) %all-reduce.2.cloned.1.call-update) | async-done | bytes 524304 | tf_op jit(solution)/shard_map/psum | solution.py:110
  91.0 0.9 add_convert_fusion
  92.1 0.3 convolution_convert_fusion.1
  92.4 10.7 %all_to_all.10 = bf16[4,16,2048]{2,1,0:T(8,128)(2,1)S(1)} all-to-all(bf16[4,16,2048]{2,1,0:T(8,128)(2,1)S(1)} %bitcast.445), channel_id=1, replica_groups=mesh['ctx'=8,'exp'=4] {'exp'}, dimensions={0} | all-to-all | bytes 524288 | tf_op jit(solution)/shard_map/all_to_all | solution.py:128
  103.2 6.7 %collective-permute-done = bf16[4,16,2048]{2,1,0:T(8,128)(2,1)S(1)} collective-permute-done((bf16[4,16,2048]{2,1,0:T(8,128)(2,1)S(1)}, bf16[4,16,2048]{2,1,0:T(8,128)(2,1)S(1)}, u32[]{:S(2)}, u32[]{:S(2)}) %collective-permute-start) | collective-permute-done | bytes 262176 | tf_op jit(solution)/shard_map/ppermute | solution.py:137
  109.9 6.7 %collective-permute-done.1 = bf16[4,16,2048]{2,1,0:T(8,128)(2,1)S(1)} collective-permute-done((bf16[4,16,2048]{2,1,0:T(8,128)(2,1)S(1)}, bf16[4,16,2048]{2,1,0:T(8,128)(2,1)S(1)}, u32[]{:S(2)}, u32[]{:S(2)}) %collective-permute-start.1) | collective-permute-done | bytes 262176 | tf_op jit(solution)/shard_map/ppermute | solution.py:137
  116.6 6.7 %collective-permute-done.2 = bf16[4,16,2048]{2,1,0:T(8,128)(2,1)S(1)} collective-permute-done((bf16[4,16,2048]{2,1,0:T(8,128)(2,1)S(1)}, bf16[4,16,2048]{2,1,0:T(8,128)(2,1)S(1)}, u32[]{:S(2)}, u32[]{:S(2)}) %collective-permute-start.2) | collective-permute-done | bytes 262176 | tf_op jit(solution)/shard_map/ppermute | solution.py:137
  123.3 6.7 %collective-permute-done.3 = bf16[4,16,2048]{2,1,0:T(8,128)(2,1)S(1)} collective-permute-done((bf16[4,16,2048]{2,1,0:T(8,128)(2,1)S(1)}, bf16[4,16,2048]{2,1,0:T(8,128)(2,1)S(1)}, u32[]{:S(2)}, u32[]{:S(2)}) %collective-permute-start.3) | collective-permute-done | bytes 262176 | tf_op jit(solution)/shard_map/ppermute | solution.py:137
  130.0 6.7 %collective-permute-done.4 = bf16[4,16,2048]{2,1,0:T(8,128)(2,1)S(1)} collective-permute-done((bf16[4,16,2048]{2,1,0:T(8,128)(2,1)S(1)}, bf16[4,16,2048]{2,1,0:T(8,128)(2,1)S(1)}, u32[]{:S(2)}, u32[]{:S(2)}) %collective-permute-start.4) | collective-permute-done | bytes 262176 | tf_op jit(solution)/shard_map/ppermute | solution.py:137
  136.6 6.7 %collective-permute-done.5 = bf16[4,16,2048]{2,1,0:T(8,128)(2,1)S(1)} collective-permute-done((bf16[4,16,2048]{2,1,0:T(8,128)(2,1)S(1)}, bf16[4,16,2048]{2,1,0:T(8,128)(2,1)S(1)}, u32[]{:S(2)}, u32[]{:S(2)}) %collective-permute-start.5) | collective-permute-done | bytes 262176 | tf_op jit(solution)/shard_map/ppermute | solution.py:137
  143.3 6.7 %collective-permute-done.6 = bf16[4,16,2048]{2,1,0:T(8,128)(2,1)S(1)} collective-permute-done((bf16[4,16,2048]{2,1,0:T(8,128)(2,1)S(1)}, bf16[4,16,2048]{2,1,0:T(8,128)(2,1)S(1)}, u32[]{:S(2)}, u32[]{:S(2)}) %collective-permute-start.6) | collective-permute-done | bytes 262176 | tf_op jit(solution)/shard_map/ppermute | solution.py:137
  150.5 0.2 constant_dynamic-slice_fusion.18
  150.7 1.7 copy-done.7
  152.4 2.3 %fusion.6 = f32[512,1024]{1,0:T(8,128)S(1)} fusion(bf16[512,2048]{1,0:T(8,128)(2,1)S(1)} %bitcast.428, bf16[1,2048,1024]{2,1,0:T(8,128)(2,1)S(1)} %copy-done.7), kind=kOutput, calls=%fused_computation.61 | convolution fusion | flops 2147483648 | bytes 8388608 | tf_op jit(solution)/shard_map/dot_general | solution.py:144
  154.8 2.5 %multiply_convert_fusion = bf16[512,1024]{1,0:T(8,128)(2,1)S(1)} fusion(f32[512,1024]{1,0:T(8,128)S(1)} %fusion.6, bf16[512,2048]{1,0:T(8,128)(2,1)S(1)} %bitcast.429, bf16[1,2048,1024]{2,1,0:T(8,128)(2,1)S(1)} %copy-done.8), kind=kOutput, calls=%fused_computation.68 | convolution fusion | flops 2150629376 | bytes 9437184 | tf_op jit(solution)/shard_map/dot_general | solution.py:145
  157.4 3.7 %fusion.8 = bf16[32,16,2048]{2,1,0:T(8,128)(2,1)} fusion(bf16[32,16,1024]{2,1,0:T(8,128)(2,1)S(1)} %bitcast.515, bf16[1,1024,2048]{2,1,0:T(8,128)(2,1)S(1)} %copy-done.9), kind=kOutput, calls=%fused_computation.63 | convolution fusion | flops 2148532224 | bytes 7340032 | tf_op jit(solution)/shard_map/dot_general | solution.py:152
  161.1 39.8 %reduce-scatter.2.cloned.1.call-done = bf16[4,16,2048]{2,1,0:T(8,128)(2,1)} async-done(((bf16[32,16,2048]{2,1,0:T(8,128)(2,1)}), bf16[4,16,2048]{2,1,0:T(8,128)(2,1)}) %reduce-scatter.2.cloned.1.call-update) | async-done | bytes 262160 | tf_op jit(solution)/shard_map/reduce_scatter | solution.py:154
  200.9 4.6 %all-to-all-start.1 = ((bf16[4,16,2048]{2,1,0:T(8,128)(2,1)}), bf16[4,16,2048]{2,1,0:T(8,128)(2,1)S(1)}, u32[]{:S(2)}, u32[]{:S(2)}) async-start(bf16[4,16,2048]{2,1,0:T(8,128)(2,1)} %reduce-scatter.2.cloned.1.call-done), calls=%async_computation.2 | async-start | bytes 524288 | tf_op jit(solution)/shard_map/all_to_all | solution.py:157
  205.6 8.8 %all-to-all-done.1 = bf16[4,16,2048]{2,1,0:T(8,128)(2,1)S(1)} async-done(((bf16[4,16,2048]{2,1,0:T(8,128)(2,1)}), bf16[4,16,2048]{2,1,0:T(8,128)(2,1)S(1)}, u32[]{:S(2)}, u32[]{:S(2)}) %all-to-all-start.1) | async-done | bytes 262176 | tf_op jit(solution)/shard_map/all_to_all | solution.py:157
  214.4 0.9 fusion.11
  (279 shorter events, 10.0 us)
Async XLA Ops:
  6.5 84.5 %all-reduce.2.cloned.1.call-start = ((), (), s32[]{:S(2)}) async-start(), calls=%async_computation.3 | async-start | bytes 1048576 | tf_op jit(solution)/shard_map/psum | solution.py:110
  12.4 13.5 %copy-start.1 = (f32[16,1024]{1,0:T(8,128)S(1)}, f32[16,1024]{1,0:T(8,128)}, u32[]{:S(2)}) copy-start(f32[16,1024]{1,0:T(8,128)} %param.25) | copy-start | bytes 196612
  12.4 34.0 %copy-start = (bf16[128,1024]{1,0:T(8,128)(2,1)S(1)}, bf16[128,1024]{1,0:T(8,128)(2,1)}, u32[]{:S(2)}) copy-start(bf16[128,1024]{1,0:T(8,128)(2,1)} %param.20) | copy-start | bytes 786436
  12.4 34.0 %copy-start.10 = (bf16[128,1024]{1,0:T(8,128)(2,1)S(1)}, bf16[128,1024]{1,0:T(8,128)(2,1)}, u32[]{:S(2)}) copy-start(bf16[128,1024]{1,0:T(8,128)(2,1)} %param.21) | copy-start | bytes 786436
  12.4 34.0 %copy-start.11 = (f32[1024]{0:T(1024)S(1)}, f32[1024]{0:T(1024)}, u32[]{:S(2)}) copy-start(f32[1024]{0:T(1024)} %param.26) | copy-start | bytes 12292
  46.5 5.9 %copy-start.4 = (s32[32,2]{0,1:T(2,128)S(1)}, s32[32,2]{0,1:T(2,128)}, u32[]{:S(2)}) copy-start(s32[32,2]{0,1:T(2,128)} %param.34) | copy-start | bytes 772
  46.5 5.9 %copy-start.5 = (s32[32,2]{0,1:T(2,128)S(1)}, s32[32,2]{0,1:T(2,128)}, u32[]{:S(2)}) copy-start(s32[32,2]{0,1:T(2,128)} %param.33) | copy-start | bytes 772
  46.5 44.6 %copy-start.2 = (bf16[32,2048]{1,0:T(8,128)(2,1)S(1)}, bf16[32,2048]{1,0:T(8,128)(2,1)}, u32[]{:S(2)}) copy-start(bf16[32,2048]{1,0:T(8,128)(2,1)} %param.28) | copy-start | bytes 393220
  46.5 45.6 %copy-start.3 = (f32[2048]{0:T(1024)S(1)}, f32[2048]{0:T(1024)}, u32[]{:S(2)}) copy-start(f32[2048]{0:T(1024)} %param.29) | copy-start | bytes 24580
  52.3 148.6 %reduce-scatter.2.cloned.1.call-start = ((), (), s32[]{:S(2)}) async-start(), calls=%async_computation.4 | async-start | bytes 2359296 | tf_op jit(solution)/shard_map/reduce_scatter | solution.py:154
  103.2 6.7 %collective-permute-start = (bf16[4,16,2048]{2,1,0:T(8,128)(2,1)S(1)}, bf16[4,16,2048]{2,1,0:T(8,128)(2,1)S(1)}, u32[]{:S(2)}, u32[]{:S(2)}) collective-permute-start(bf16[4,16,2048]{2,1,0:T(8,128)(2,1)S(1)} %all_to_all.10), channel_id=1, source_target_pairs={{0,4},{4,8},{8,12},{12,16},{16,20},{20,24},{24,28},{28,0},{1,5},{5... | collective-permute-start | bytes 786440 | tf_op jit(solution)/shard_map/ppermute | solution.py:137
  109.9 6.7 %collective-permute-start.1 = (bf16[4,16,2048]{2,1,0:T(8,128)(2,1)S(1)}, bf16[4,16,2048]{2,1,0:T(8,128)(2,1)S(1)}, u32[]{:S(2)}, u32[]{:S(2)}) collective-permute-start(bf16[4,16,2048]{2,1,0:T(8,128)(2,1)S(1)} %collective-permute-done), channel_id=1, source_target_pairs={{0,4},{4,8},{8,12},{12,16},{16,20},{20,24},{24,28},{28,0},{1,5},{5... | collective-permute-start | bytes 786440 | tf_op jit(solution)/shard_map/ppermute | solution.py:137
  116.6 6.7 %collective-permute-start.2 = (bf16[4,16,2048]{2,1,0:T(8,128)(2,1)S(1)}, bf16[4,16,2048]{2,1,0:T(8,128)(2,1)S(1)}, u32[]{:S(2)}, u32[]{:S(2)}) collective-permute-start(bf16[4,16,2048]{2,1,0:T(8,128)(2,1)S(1)} %collective-permute-done.1), channel_id=1, source_target_pairs={{0,4},{4,8},{8,12},{12,16},{16,20},{20,24},{24,28},{28,0},{1,5},{5... | collective-permute-start | bytes 786440 | tf_op jit(solution)/shard_map/ppermute | solution.py:137
  123.3 6.7 %collective-permute-start.3 = (bf16[4,16,2048]{2,1,0:T(8,128)(2,1)S(1)}, bf16[4,16,2048]{2,1,0:T(8,128)(2,1)S(1)}, u32[]{:S(2)}, u32[]{:S(2)}) collective-permute-start(bf16[4,16,2048]{2,1,0:T(8,128)(2,1)S(1)} %collective-permute-done.2), channel_id=1, source_target_pairs={{0,4},{4,8},{8,12},{12,16},{16,20},{20,24},{24,28},{28,0},{1,5},{5... | collective-permute-start | bytes 786440 | tf_op jit(solution)/shard_map/ppermute | solution.py:137
  129.9 6.7 %collective-permute-start.4 = (bf16[4,16,2048]{2,1,0:T(8,128)(2,1)S(1)}, bf16[4,16,2048]{2,1,0:T(8,128)(2,1)S(1)}, u32[]{:S(2)}, u32[]{:S(2)}) collective-permute-start(bf16[4,16,2048]{2,1,0:T(8,128)(2,1)S(1)} %collective-permute-done.3), channel_id=1, source_target_pairs={{0,4},{4,8},{8,12},{12,16},{16,20},{20,24},{24,28},{28,0},{1,5},{5... | collective-permute-start | bytes 786440 | tf_op jit(solution)/shard_map/ppermute | solution.py:137
  136.6 6.7 %collective-permute-start.5 = (bf16[4,16,2048]{2,1,0:T(8,128)(2,1)S(1)}, bf16[4,16,2048]{2,1,0:T(8,128)(2,1)S(1)}, u32[]{:S(2)}, u32[]{:S(2)}) collective-permute-start(bf16[4,16,2048]{2,1,0:T(8,128)(2,1)S(1)} %collective-permute-done.4), channel_id=1, source_target_pairs={{0,4},{4,8},{8,12},{12,16},{16,20},{20,24},{24,28},{28,0},{1,5},{5... | collective-permute-start | bytes 786440 | tf_op jit(solution)/shard_map/ppermute | solution.py:137
  143.3 6.7 %collective-permute-start.6 = (bf16[4,16,2048]{2,1,0:T(8,128)(2,1)S(1)}, bf16[4,16,2048]{2,1,0:T(8,128)(2,1)S(1)}, u32[]{:S(2)}, u32[]{:S(2)}) collective-permute-start(bf16[4,16,2048]{2,1,0:T(8,128)(2,1)S(1)} %collective-permute-done.5), channel_id=1, source_target_pairs={{0,4},{4,8},{8,12},{12,16},{16,20},{20,24},{24,28},{28,0},{1,5},{5... | collective-permute-start | bytes 786440 | tf_op jit(solution)/shard_map/ppermute | solution.py:137
  150.3 2.2 copy-start.7
  152.4 2.4 %copy-start.8 = (bf16[1,2048,1024]{2,1,0:T(8,128)(2,1)S(1)}, bf16[1,2048,1024]{2,1,0:T(8,128)(2,1)}, u32[]{:S(2)}) copy-start(bf16[1,2048,1024]{2,1,0:T(8,128)(2,1)} %param.31) | copy-start | bytes 12582916
  154.8 2.5 %copy-start.9 = (bf16[1,1024,2048]{2,1,0:T(8,128)(2,1)S(1)}, bf16[1,1024,2048]{2,1,0:T(8,128)(2,1)}, u32[]{:S(2)}) copy-start(bf16[1,1024,2048]{2,1,0:T(8,128)(2,1)} %param.32) | copy-start | bytes 12582916
  157.4 48.1 %copy-start.6 = (f32[32,2]{0,1:T(2,128)S(1)}, f32[32,2]{0,1:T(2,128)}, u32[]{:S(2)}) copy-start(f32[32,2]{0,1:T(2,128)} %param.35) | copy-start | bytes 772
  200.9 13.5 %all-to-all-start.1 = ((bf16[4,16,2048]{2,1,0:T(8,128)(2,1)}), bf16[4,16,2048]{2,1,0:T(8,128)(2,1)S(1)}, u32[]{:S(2)}, u32[]{:S(2)}) async-start(bf16[4,16,2048]{2,1,0:T(8,128)(2,1)} %reduce-scatter.2.cloned.1.call-done), calls=%async_computation.2 | async-start | bytes 524288 | tf_op jit(solution)/shard_map/all_to_all | solution.py:157
Sparse Core Ops, SparseCore 0:
  52.4 38.5 all-reduce.1
  161.2 39.6 reduce-scatter.1
